TPU v7x, 256 devices: a whole 4x4x8 slice. The times are simulated.
256 devices in a mesh: section: 16 (over x_lo, y, core), dp: 16 (over x_hi, z).
Axes of the slice: x: 4 (x_hi: 2, x_lo: 2; x = x_hi * 2 + x_lo), y: 4, z: 8, core: 2. Of those that a mesh axis runs over, the one named last changes fastest.
Arguments:
- activations: bfloat16 [16, 16, 256, 4096], P('section', 'dp'), may hold values from -6 to 6
- gains: float32 [2, 16, 4096], P(None, 'section'), may hold values from 0.1 to 1.9
- kv_weight: bfloat16 [2, 16, 4096, 1024], P(None, 'section', 'dp'), as said below
- lengths: int32 [16, 16], P('section', 'dp'), may hold values from 64 to 256
Outputs:
- advanced: bfloat16 [16, 16, 256, 4096], P('section', 'dp')
Inputs may be any that keep to these rules, and one draw needn't show every extreme that they name: `kv_weight`: projection weights of order one to eight over square root of 4096.
All inputs are finite; a program needn't handle non-finite values.
Results may differ from a plain program's by a relative error of at most 0.022.
Values may be sent and summed in bfloat16 or wider, within the bound.
A program may use at most 128 MiB of HBM per device.

v0:
```python
import jax
import jax.numpy as jnp
from jax import lax
from jax.sharding import PartitionSpec as P

HEAD_DIM = 128
TICKS = 3


def from_behind(shard, axis, by):
    peers = lax.axis_size(axis)
    return lax.ppermute(shard, axis, [(i, (i + by) % peers) for i in range(peers)])


def normalize(block, gain):
    xf = block.astype(jnp.float32)
    factor = lax.rsqrt(jnp.mean(xf * xf, axis=-1, keepdims=True) + 1e-05)
    return (xf, (xf * factor * gain).astype(jnp.bfloat16))


def finish(xf, normed, keyval, length):
    seq = normed.shape[0]
    width = keyval.shape[1] // 2
    groups = width // HEAD_DIM
    keys = keyval[:, :width].reshape(seq, groups, HEAD_DIM)
    values = keyval[:, width:].reshape(seq, groups, HEAD_DIM)
    query = normed.reshape(seq, groups, -1, HEAD_DIM)
    scores = jnp.einsum(
        "qhgd,khd->hgqk", query, keys, preferred_element_type=jnp.float32
    ) * HEAD_DIM ** (-0.5)
    places = jnp.arange(seq, dtype=jnp.int32)
    allowed = (places[None, :] <= places[:, None]) & (places[None, :] < length)
    scores = jnp.where(allowed, scores, -1e30)
    topmost = jnp.max(scores, axis=-1, keepdims=True)
    expo = jnp.exp(scores - topmost)
    probs = (expo / jnp.sum(expo, axis=-1, keepdims=True)).astype(jnp.bfloat16)
    mixed = jnp.einsum("hgqk,khd->qhgd", probs, values, preferred_element_type=jnp.float32).reshape(
        seq, -1
    )
    return (xf + mixed).astype(jnp.bfloat16)


def per_device(activations, gains, kv_weight, lengths):
    block = activations[0, 0]
    length = lengths[0, 0]
    section = lax.axis_index("section")
    local_rows = kv_weight[:, 0]
    gain_rows = gains[:, 0]
    for tick in range(TICKS):
        repeat = (section < tick).astype(jnp.int32)
        gain = lax.dynamic_index_in_dim(gain_rows, repeat, 0, keepdims=False)
        xf, normed = normalize(block, gain)
        shard_rows = lax.dynamic_index_in_dim(local_rows, repeat, 0, keepdims=False)

        def add_rows(total, piece, start, normed=normed):
            return jnp.dot(normed, piece, preferred_element_type=jnp.float32)

        empty = jnp.zeros((normed.shape[0], shard_rows.shape[1]), jnp.float32)
        keyval = add_rows(empty, lax.all_gather(shard_rows, "dp", axis=0, tiled=True), jnp.int32(0))
        block = finish(xf, normed, keyval.astype(jnp.bfloat16), length)
        block, length = from_behind((block, length), "section", 1)
    return block[None, None]


def solution(mesh):
    return jax.shard_map(
        per_device,
        mesh=mesh,
        in_specs=(
            P("section", "dp", None, None),
            P(None, "section", None),
            P(None, "section", "dp", None),
            P("section", "dp"),
        ),
        out_specs=P("section", "dp", None, None),
        check_vma=False,
    )
```

profile of v0, /device:TPU:8, one launch (start us, length us, event | category | flops | bytes accessed | tf_op | source)
XLA Modules:
  0.0 475.0 jit_solution(14156711579204725986)
XLA Ops:
  6.5 2.8 constant_dynamic-slice_fusion.4
  12.5 2.7 copy.38
  15.4 133.3 %all-gather.7.cloned.1.call-done = bf16[1,1,4096,1024]{3,2,1,0:T(8,128)(2,1)} async-done(((bf16[1,1,256,1024]{3,2,1,0:T(8,128)(2,1)}), bf16[1,1,4096,1024]{3,2,1,0:T(8,128)(2,1)}) %all-gather.7.cloned.1.call-update) | async-done | bytes 8388624 | tf_op jit(solution)/shard_map/all_gather | solution.py:59
  148.7 5.8 %fusion.52 = bf16[256,1024]{1,0:T(8,128)(2,1)S(1)} fusion(bf16[1,1,4096,1024]{3,2,1,0:T(8,128)(2,1)} %all-gather.7.cloned.1.call-done, bf16[1,1,256,4096]{3,2,1,0:T(8,128)(2,1)S(1)} %copy-done, f32[4096]{0:T(1024)S(1)} %bitcast.131, f32[256]{0:T(256)S(1)} %add_rsqrt_fusion.2), kind=kOutput, calls=%fused_computation.68 | convolution fusion | flops 2151940096 | bytes 11027456 | tf_op jit(solution)/shard_map/dot_general | solution.py:56
  154.7 5.2 %fusion.41 = f32[4,256,256,8]{2,1,3,0:T(8,128)S(1)} fusion(f32[256,4,8,128]{3,2,1,0:T(8,128)} %bitcast.118, f32[4,8,128]{2,1,0:T(8,128)S(1)} %bitcast.132, f32[256]{0:T(256)S(1)} %add_rsqrt_fusion.2, bf16[256,4,128,1]{2,1,0,3:T(4,128)(2,1)S(1)} %bitcast.125), kind=kOutput, calls=%fused_computation.59 | convolution fusion | flops 540016640 | bytes 12862464 | tf_op jit(solution)/shard_map/qhgd,khd->hgqk/dot_general | solution.py:28
  159.9 2.4 fusion.82
  162.3 2.7 fusion.35
  165.0 5.6 %copy.9 = f32[256,4096]{1,0:T(8,128)} copy(f32[256,4096]{0,1:T(8,128)} %bitcast.121) | data formatting | bytes 8388608 | tf_op jit(solution)/shard_map/reshape | solution.py:37
  170.6 2.8 fusion.18
  173.5 1.6 collective-permute-start.1
  175.1 24.0 %collective-permute-done.1 = s32[]{:T(128)} collective-permute-done((s32[]{:T(128)}, s32[]{:T(128)}, u32[]{:S(2)}, u32[]{:S(2)}) %collective-permute-start.1) | collective-permute-done | bytes 36 | tf_op jit(solution)/shard_map/ppermute | solution.py:12
  201.1 1.8 copy.39
  202.9 81.0 %all-gather.9.cloned.1.call-done = bf16[1,1,4096,1024]{3,2,1,0:T(8,128)(2,1)} async-done(((bf16[1,1,256,1024]{3,2,1,0:T(8,128)(2,1)}), bf16[1,1,4096,1024]{3,2,1,0:T(8,128)(2,1)}) %all-gather.9.cloned.1.call-update) | async-done | bytes 8388624 | tf_op jit(solution)/shard_map/all_gather | solution.py:59
  283.9 5.7 %fusion.57 = bf16[256,1024]{1,0:T(8,128)(2,1)S(1)} fusion(bf16[1,1,4096,1024]{3,2,1,0:T(8,128)(2,1)} %all-gather.9.cloned.1.call-done, bf16[256,4096]{1,0:T(8,128)(2,1)S(1)} %collective-permute-done, f32[4096]{0:T(1024)S(1)} %bitcast.136, f32[256]{0:T(256)S(1)} %add_rsqrt_fusion.1), kind=kOutput, calls=%fused_computation.69 | convolution fusion | flops 2151940096 | bytes 11027456 | tf_op jit(solution)/shard_map/dot_general | solution.py:56
  289.9 2.9 fusion.46
  292.9 2.4 fusion.83
  295.2 2.8 fusion.36
  298.0 5.6 %copy.14 = f32[256,4096]{1,0:T(8,128)} copy(f32[256,4096]{0,1:T(8,128)} %bitcast.122) | data formatting | bytes 8388608 | tf_op jit(solution)/shard_map/reshape | solution.py:37
  303.7 2.8 fusion.22
  306.5 1.6 collective-permute-start.3
  308.1 24.0 %collective-permute-done.3 = s32[]{:T(128)} collective-permute-done((s32[]{:T(128)}, s32[]{:T(128)}, u32[]{:S(2)}, u32[]{:S(2)}) %collective-permute-start.3) | collective-permute-done | bytes 36 | tf_op jit(solution)/shard_map/ppermute | solution.py:12
  333.3 0.8 fusion.63
  334.1 1.8 copy.40
  335.9 83.3 %all-gather.11.cloned.1.call-done = bf16[1,1,4096,1024]{3,2,1,0:T(8,128)(2,1)} async-done(((bf16[1,1,256,1024]{3,2,1,0:T(8,128)(2,1)}), bf16[1,1,4096,1024]{3,2,1,0:T(8,128)(2,1)}) %all-gather.11.cloned.1.call-update) | async-done | bytes 8388624 | tf_op jit(solution)/shard_map/all_gather | solution.py:59
  419.2 5.8 %fusion.60 = bf16[256,1024]{1,0:T(8,128)(2,1)S(1)} fusion(bf16[1,1,4096,1024]{3,2,1,0:T(8,128)(2,1)} %all-gather.11.cloned.1.call-done, bf16[256,4096]{1,0:T(8,128)(2,1)S(1)} %collective-permute-done.2, f32[4096]{0:T(1024)S(1)} %bitcast.134, f32[256]{0:T(256)S(1)} %add_rsqrt_fusion), kind=kOutput, calls=%fused_computation.70 | convolution fusion | flops 2151940096 | bytes 11027456 | tf_op jit(solution)/shard_map/dot_general | solution.py:56
  425.2 2.9 fusion.44
  428.1 2.4 fusion.84
  430.5 2.7 fusion.37
  433.2 5.6 %copy.19 = f32[256,4096]{1,0:T(8,128)} copy(f32[256,4096]{0,1:T(8,128)} %bitcast.123) | data formatting | bytes 8388608 | tf_op jit(solution)/shard_map/reshape | solution.py:37
  438.9 2.7 fusion.26
  441.7 25.4 %collective-permute-done.4 = bf16[256,4096]{1,0:T(8,128)(2,1)S(1)} collective-permute-done((bf16[256,4096]{1,0:T(8,128)(2,1)S(1)}, bf16[256,4096]{1,0:T(8,128)(2,1)S(1)}, u32[]{:S(2)}, u32[]{:S(2)}) %collective-permute-start.4) | collective-permute-done | bytes 2097184 | tf_op jit(solution)/shard_map/ppermute | solution.py:12
  467.2 1.3 copy.59
  (39 shorter events, 6.7 us)
Async XLA Ops:
  6.5 4.3 copy-start
  6.5 142.1 %all-gather.7.cloned.1.call-start = ((), (), s32[]{:S(2)}) async-start(), calls=%async_computation | async-start | bytes 8912896 | tf_op jit(solution)/shard_map/all_gather | solution.py:59
  9.4 274.6 %all-gather.9.cloned.1.call-start = ((), (), s32[]{:S(2)}) async-start(), calls=%async_computation.1 | async-start | bytes 8912896 | tf_op jit(solution)/shard_map/all_gather | solution.py:59
  10.1 409.1 %all-gather.11.cloned.1.call-start = ((), (), s32[]{:S(2)}) async-start(), calls=%async_computation.2 | async-start | bytes 8912896 | tf_op jit(solution)/shard_map/all_gather | solution.py:59
  12.5 2.8 copy-start.1
  173.4 26.4 %collective-permute-start = (bf16[256,4096]{1,0:T(8,128)(2,1)S(1)}, bf16[256,4096]{1,0:T(8,128)(2,1)S(1)}, u32[]{:S(2)}, u32[]{:S(2)}) collective-permute-start(bf16[256,4096]{1,0:T(8,128)(2,1)S(1)} %fusion.18), channel_id=1, source_target_pairs={{0,16},{16,32},{32,48},{48,64},{64,80},{80,96},{96,112},{112,128},... | collective-permute-start | bytes 6291464 | tf_op jit(solution)/shard_map/ppermute | solution.py:12
  173.5 25.6 %collective-permute-start.1 = (s32[]{:T(128)}, s32[]{:T(128)}, u32[]{:S(2)}, u32[]{:S(2)}) collective-permute-start(s32[]{:T(128)} %bitcast.6), channel_id=1, source_target_pairs={{0,16},{16,32},{32,48},{48,64},{64,80},{80,96},{96,112},{112,128},... | collective-permute-start | bytes 20 | tf_op jit(solution)/shard_map/ppermute | solution.py:12
  306.4 26.4 %collective-permute-start.2 = (bf16[256,4096]{1,0:T(8,128)(2,1)S(1)}, bf16[256,4096]{1,0:T(8,128)(2,1)S(1)}, u32[]{:S(2)}, u32[]{:S(2)}) collective-permute-start(bf16[256,4096]{1,0:T(8,128)(2,1)S(1)} %fusion.22), channel_id=1, source_target_pairs={{0,16},{16,32},{32,48},{48,64},{64,80},{80,96},{96,112},{112,128},... | collective-permute-start | bytes 6291464 | tf_op jit(solution)/shard_map/ppermute | solution.py:12
  306.5 25.6 %collective-permute-start.3 = (s32[]{:T(128)}, s32[]{:T(128)}, u32[]{:S(2)}, u32[]{:S(2)}) collective-permute-start(s32[]{:T(128)} %collective-permute-done.1), channel_id=1, source_target_pairs={{0,16},{16,32},{32,48},{48,64},{64,80},{80,96},{96,112},{112,128},... | collective-permute-start | bytes 20 | tf_op jit(solution)/shard_map/ppermute | solution.py:12
  441.6 25.5 %collective-permute-start.4 = (bf16[256,4096]{1,0:T(8,128)(2,1)S(1)}, bf16[256,4096]{1,0:T(8,128)(2,1)S(1)}, u32[]{:S(2)}, u32[]{:S(2)}) collective-permute-start(bf16[256,4096]{1,0:T(8,128)(2,1)S(1)} %fusion.26), channel_id=1, source_target_pairs={{0,16},{16,32},{32,48},{48,64},{64,80},{80,96},{96,112},{112,128},... | collective-permute-start | bytes 6291464 | tf_op jit(solution)/shard_map/ppermute | solution.py:12
Sparse Core Ops, SparseCore 0:
  9.9 138.6 all-gather.6
  151.3 132.6 all-gather.8
  286.5 132.6 all-gather.10
where the time goes:
time: 477 us; the launch traced here: 475 us
  waiting for transfers between devices  372 us (78%)
  matrix products  36.6 us (8%)
  local copies, waits for them, and re-layouts  28.1 us (6%)
  other arithmetic  20.3 us (4%)
  between operations  14 us (3%)
    all_gather x3, waiting for transfers between devices, per_device(): lax.all_gather(shard_rows, 'dp', axis=0, tiled=True)  298 us
    ppermute x5, waiting for transfers between devices, from_behind(): lax.ppermute(shard, axis, [(i, (i + by) % peers) for i in range(peers)])  73.5 us
    dot_general x3, matrix products, add_rows(): return jnp.dot(normed, piece, preferred_element_type=jnp.float32)  17.3 us
    reshape x3, local copies, waits for them, and re-layouts, finish(): jnp.einsum('hgqk,khd->qhgd', probs, values, preferred_element_type=jnp.fl...  16.9 us
    dot_general x3, matrix products, finish(): jnp.einsum('qhgd,khd->hgqk', query, keys, preferred_element_type=jnp.floa...  11.1 us
  transfers between devices with their start and end apart: 8, of which 6 were waited for; matrix products, arithmetic and copies ran while one was open for 12% of the time, Pallas kernels for 0%

commit v1 on v0

v1 whole, which is shorter than its diff:
```python
import functools
import math

import jax
import jax.numpy as jnp
from jax import lax
from jax.experimental import pallas as pl
from jax.experimental.pallas import tpu as pltpu
from jax.sharding import PartitionSpec as P

HEAD_DIM = 128
TICKS = 3
RING = 8
KV_HEADS = 4
PER_KV = 8
MESH = pl.DeviceIdType.MESH
SCALE2 = HEAD_DIM ** (-0.5) * math.log2(math.e)


def kernel(
    x_hbm, gains_hbm, w_hbm, len_ref, out_hbm,
    wbuf, stage, xbuf, nbuf, gbuf, lbuf, lown, bias, kbuf, vbuf,
    stage_sem, ring_send, ring_recv, seed_send, x_send, x_recv,
    g_send, g_recv, l_send, l_recv, out_sem,
):
    sections = lax.axis_size("section")
    sec = lax.axis_index("section")
    dp = lax.axis_index("dp")
    z = lax.rem(dp, RING)
    base = dp - z
    seq = xbuf.shape[2]
    cols = xbuf.shape[3]
    rows = stage.shape[2]
    nxt = lax.rem(sec + 1, sections)
    prv = lax.rem(sec + sections - 1, sections)
    across = RING - base + z
    up = base + lax.rem(z + 1, RING)
    down = base + lax.rem(z + RING - 1, RING)
    gives_second = sec <= 1
    has_second = (sec == 1) | (sec == 2)

    def stage_copy(r, h, part):
        return pltpu.make_async_copy(
            w_hbm.at[r, 0, :, pl.ds(part * KV_HEADS * HEAD_DIM + h * HEAD_DIM, HEAD_DIM)],
            stage.at[r, h, :, pl.ds(part * HEAD_DIM, HEAD_DIM)],
            stage_sem.at[r, h, part],
        )

    for h in range(KV_HEADS):
        for part in range(2):
            stage_copy(0, h, part).start()

    @pl.when(gives_second)
    def _():
        for h in range(KV_HEADS):
            for part in range(2):
                stage_copy(1, h, part).start()

    lown[...] = jnp.full(lown.shape, len_ref[0, 0], jnp.int32)

    barrier = pltpu.get_barrier_semaphore()
    for peer in ((nxt, dp), (nxt, across), (prv, dp), (prv, across), (sec, up), (sec, down)):
        pl.semaphore_signal(barrier, inc=1, device_id=peer, device_id_type=MESH)
    pl.semaphore_wait(barrier, 6)

    def block(ref, r, h, blk):
        return ref.at[r, h, pl.ds(pl.multiple_of(blk * rows, rows), rows), :]

    def seed(r, h, side):
        return pltpu.make_async_remote_copy(
            src_ref=stage.at[r, h],
            dst_ref=block(wbuf, r, h, dp),
            send_sem=seed_send.at[r, h, side],
            recv_sem=ring_recv.at[r, h, dp],
            device_id=(nxt, across if side else dp),
            device_id_type=MESH,
        )

    def ring(r, h, half, k, way):
        blk = half * RING + lax.rem(z + (k if way else RING - k), RING)
        return pltpu.make_async_remote_copy(
            src_ref=block(wbuf, r, h, blk),
            dst_ref=block(wbuf, r, h, blk),
            send_sem=ring_send.at[r, way, h, half, k],
            recv_sem=ring_recv.at[r, h, blk],
            device_id=(sec, down if way else up),
            device_id_type=MESH,
        )

    def step(r, group, k):
        def one(q, carry):
            h = group * 2 + q // 2
            half = lax.rem(q, 2)
            if k == 0:
                ring(r, h, half, 0, 0).wait_recv()
                ring(r, h, half, 0, 0).start()
                ring(r, h, half, 0, 1).start()
            elif k < 3:
                ring(r, h, half, k, 0).wait_recv()
                ring(r, h, half, k, 0).start()
                ring(r, h, half, k, 1).wait_recv()
                ring(r, h, half, k, 1).start()
            elif k == 3:
                ring(r, h, half, k, 0).wait_recv()

                @pl.when(lax.rem(h, 2) == 0)
                def _():
                    ring(r, h, half, k, 0).start()

                ring(r, h, half, k, 1).wait_recv()

                @pl.when(lax.rem(h, 2) == 1)
                def _():
                    ring(r, h, half, k, 1).start()
            else:
                ring(r, h, half, k, 0).wait_recv()
            return carry

        lax.fori_loop(0, 4, one, 0)

    def ring_done(r):
        def one(q, carry):
            h = q // 2
            half = lax.rem(q, 2)
            for k in range(3):
                ring(r, h, half, k, 0).wait_send()
                ring(r, h, half, k, 1).wait_send()

            @pl.when(lax.rem(h, 2) == 0)
            def _():
                ring(r, h, half, 3, 0).wait_send()

            @pl.when(lax.rem(h, 2) == 1)
            def _():
                ring(r, h, half, 3, 1).wait_send()

            return carry

        lax.fori_loop(0, 2 * KV_HEADS, one, 0)

    def first_x(c):
        return pltpu.make_async_remote_copy(
            src_ref=x_hbm.at[0, 0, :, pl.ds(c * cols, cols)],
            dst_ref=xbuf.at[0, c],
            send_sem=x_send.at[0, c],
            recv_sem=x_recv.at[0, c],
            device_id=(nxt, dp),
            device_id_type=MESH,
        )

    def shift_x(t, c):
        return pltpu.make_async_remote_copy(
            src_ref=xbuf.at[jnp.maximum(t - 1, 0), c],
            dst_ref=xbuf.at[t, c],
            send_sem=x_send.at[t, c],
            recv_sem=x_recv.at[t, c],
            device_id=(nxt, dp),
            device_id_type=MESH,
        )

    def shift_len(t, src):
        return pltpu.make_async_remote_copy(
            src_ref=src,
            dst_ref=lbuf.at[t],
            send_sem=l_send.at[t],
            recv_sem=l_recv.at[t],
            device_id=(nxt, dp),
            device_id_type=MESH,
        )

    move_gains = pltpu.make_async_remote_copy(
        src_ref=gains_hbm, dst_ref=gbuf, send_sem=g_send, recv_sem=g_recv,
        device_id=(nxt, dp), device_id_type=MESH,
    )

    def write(c):
        return pltpu.make_async_copy(
            xbuf.at[TICKS - 1, c],
            out_hbm.at[0, 0, :, pl.ds(pl.multiple_of(c * cols, cols), cols)],
            out_sem.at[c],
        )

    for h in range(KV_HEADS):
        for part in range(2):
            stage_copy(0, h, part).wait()
        seed(0, h, 0).start()
        seed(0, h, 1).start()
    move_gains.start()
    shift_len(0, lown).start()
    for c in range(KV_HEADS):
        first_x(c).start()

    @pl.when(gives_second)
    def _():
        for h in range(KV_HEADS):
            for part in range(2):
                stage_copy(1, h, part).wait()
            seed(1, h, 0).start()
            seed(1, h, 1).start()

    vbuf[:, HEAD_DIM:] = jnp.ones((seq, HEAD_DIM), jnp.bfloat16)

    step(0, 0, 0)
    step(0, 0, 1)
    step(0, 0, 2)
    step(0, 1, 0)
    step(0, 0, 3)
    move_gains.wait_recv()

    def one_head(i, carry):
        t = i // KV_HEADS
        h = lax.rem(i, KV_HEADS)
        r = ((sec >= 1) & (t >= sec)).astype(jnp.int32)

        @pl.when(i == 1)
        def _():
            step(0, 1, 2)

        @pl.when(i == 2)
        def _():
            step(0, 1, 3)

            @pl.when(has_second)
            def _():
                step(1, 0, 0)
                step(1, 1, 0)

            step(0, 1, 4)

        @pl.when((i == KV_HEADS) & has_second)
        def _():
            step(1, 0, 1)
            step(1, 1, 1)

        @pl.when(((i == KV_HEADS) & (sec == 1)) | ((i == 2 * KV_HEADS) & (sec == 2)))
        def _():
            for k in range(2, 5):
                step(1, 0, k)
                step(1, 1, k)

        @pl.when(h == 0)
        def _():
            shift_len(t, lown).wait_recv()

            @pl.when(t < TICKS - 1)
            def _():
                shift_len(t + 1, lbuf.at[t]).start()

            for c in range(KV_HEADS):
                shift_x(t, c).wait_recv()

            places = lax.broadcasted_iota(jnp.int32, (seq, seq), 0)
            keys = lax.broadcasted_iota(jnp.int32, (seq, seq), 1)
            allowed = (keys <= places) & (keys < lbuf[t][0:1, :])
            bias[...] = jnp.where(allowed, 0.0, -1e30)

            def norm_rows(b, carry):
                at = pl.ds(pl.multiple_of(b * 32, 32), 32)
                total = jnp.zeros((32, HEAD_DIM), jnp.float32)
                for c in range(KV_HEADS):
                    xf = xbuf[t, c, at, :].astype(jnp.float32)
                    sq = xf * xf
                    for g in range(cols // HEAD_DIM):
                        total = total + sq[:, g * HEAD_DIM:(g + 1) * HEAD_DIM]
                mean = jnp.sum(total, axis=-1, keepdims=True) / (cols * KV_HEADS)
                factor = lax.rsqrt(mean + 1e-05)
                for c in range(KV_HEADS):
                    xf = xbuf[t, c, at, :].astype(jnp.float32)
                    gain = gbuf[r, 0:1, c * cols:(c + 1) * cols]
                    nbuf[at, c * cols:(c + 1) * cols] = (xf * factor * gain).astype(jnp.bfloat16)
                return carry

            lax.fori_loop(0, seq // 32, norm_rows, 0)

        @pl.when(i == 0)
        def _():
            step(0, 0, 4)
            step(0, 1, 1)

        keyval = jnp.dot(nbuf[...], wbuf[r, h], preferred_element_type=jnp.float32)
        kbuf[...] = keyval[:, :HEAD_DIM].astype(jnp.bfloat16)
        vbuf[:, :HEAD_DIM] = keyval[:, HEAD_DIM:].astype(jnp.bfloat16)

        def heads(pair, carry):
            for jj in range(4):
                j = pair * 4 + jj
                at = pl.ds(pl.multiple_of(h * cols + j * HEAD_DIM, HEAD_DIM), HEAD_DIM)
                put = pl.ds(pl.multiple_of(j * HEAD_DIM, HEAD_DIM), HEAD_DIM)
                for half in range(2):
                    mine = slice(half * seq // 2, (half + 1) * seq // 2)
                    seen = (half + 1) * seq // 2
                    scores = lax.dot_general(
                        nbuf[mine, at], kbuf[:seen, :], (((1,), (1,)), ((), ())),
                        preferred_element_type=jnp.float32,
                    ) + bias[mine, :seen]
                    top = jnp.max(scores, axis=-1, keepdims=True)
                    expo = jnp.exp2((scores - top) * SCALE2).astype(jnp.bfloat16)
                    both = jnp.dot(expo, vbuf[:seen, :], preferred_element_type=jnp.float32)
                    mixed = both[:, :HEAD_DIM] / both[:, HEAD_DIM:]
                    old = xbuf[t, h, mine, put].astype(jnp.float32)
                    xbuf[t, h, mine, put] = (old + mixed).astype(jnp.bfloat16)
            return carry

        lax.fori_loop(0, PER_KV // 4, heads, 0)

        @pl.when(t < TICKS - 1)
        def _():
            shift_x(t + 1, h).start()

        @pl.when(t == TICKS - 1)
        def _():
            write(h).start()

        return carry

    lax.fori_loop(0, TICKS * KV_HEADS, one_head, 0)

    move_gains.wait_send()
    for t in range(TICKS):
        shift_len(t, lown).wait_send()
    for c in range(KV_HEADS):
        first_x(c).wait_send()
        shift_x(1, c).wait_send()
        shift_x(2, c).wait_send()
    for h in range(KV_HEADS):
        seed(0, h, 0).wait_send()
        seed(0, h, 1).wait_send()
    ring_done(0)

    @pl.when(gives_second)
    def _():
        for h in range(KV_HEADS):
            seed(1, h, 0).wait_send()
            seed(1, h, 1).wait_send()

    @pl.when(has_second)
    def _():
        ring_done(1)

    for c in range(KV_HEADS):
        write(c).wait()


def per_device(activations, gains, kv_weight, lengths):
    seq, width = activations.shape[2:]
    rows = kv_weight.shape[2]
    blocks = lax.axis_size("dp")
    cols = width // KV_HEADS
    dma = pltpu.SemaphoreType.DMA
    return pl.pallas_call(
        kernel,
        out_shape=jax.ShapeDtypeStruct(activations.shape, activations.dtype),
        in_specs=[
            pl.BlockSpec(memory_space=pl.ANY),
            pl.BlockSpec(memory_space=pl.ANY),
            pl.BlockSpec(memory_space=pl.ANY),
            pl.BlockSpec(memory_space=pltpu.SMEM),
        ],
        out_specs=pl.BlockSpec(memory_space=pl.ANY),
        scratch_shapes=[
            pltpu.VMEM((2, KV_HEADS, blocks * rows, 2 * HEAD_DIM), jnp.bfloat16),
            pltpu.VMEM((2, KV_HEADS, rows, 2 * HEAD_DIM), jnp.bfloat16),
            pltpu.VMEM((TICKS, KV_HEADS, seq, cols), jnp.bfloat16),
            pltpu.VMEM((seq, width), jnp.bfloat16),
            pltpu.VMEM(gains.shape, jnp.float32),
            pltpu.VMEM((TICKS, 8, seq), jnp.int32),
            pltpu.VMEM((8, seq), jnp.int32),
            pltpu.VMEM((seq, seq), jnp.float32),
            pltpu.VMEM((seq, HEAD_DIM), jnp.bfloat16),
            pltpu.VMEM((seq, 2 * HEAD_DIM), jnp.bfloat16),
            dma((2, KV_HEADS, 2)),
            dma((2, 2, KV_HEADS, 2, 5)),
            dma((2, KV_HEADS, blocks)),
            dma((2, KV_HEADS, 2)),
            dma((TICKS, KV_HEADS)),
            dma((TICKS, KV_HEADS)),
            dma, dma,
            dma((TICKS,)),
            dma((TICKS,)),
            dma((KV_HEADS,)),
        ],
        compiler_params=pltpu.CompilerParams(
            collective_id=0, has_side_effects=True, vmem_limit_bytes=56 * 1024 * 1024
        ),
        name="relay",
    )(activations, gains, kv_weight, lengths)


def solution(mesh):
    return jax.shard_map(
        per_device,
        mesh=mesh,
        in_specs=(
            P("section", "dp", None, None),
            P(None, "section", None),
            P(None, "section", "dp", None),
            P("section", "dp"),
        ),
        out_specs=P("section", "dp", None, None),
        check_vma=False,
    )
```

time: 477 us -> 182 us (0.38)
  waiting for transfers between devices: 372 us -> 0 us
  Pallas kernels: 0 us -> 177 us
  matrix products: 36.6 us -> 0 us
  local copies, waits for them, and re-layouts: 28.1 us -> 3.13 us
  other arithmetic: 20.3 us -> 0 us
  between operations: 14 us -> 0.66 us
    all_gather x3 -> x0, waiting for transfers between devices: 298 us -> none  [per_device(): lax.all_gather(shard_rows, 'dp', axis=0, tiled=True)]
    pallas_call x0 -> x1, Pallas kernels: none -> 177 us  [per_device(): pl.pallas_call(kernel, out_shape=jax.ShapeDtypeStruct(activations.shape,...]
    ppermute x5 -> x0, waiting for transfers between devices: 73.5 us -> none  [from_behind(): lax.ppermute(shard, axis, [(i, (i + by) % peers) for i in range(peers)])]
    dot_general x9 -> x0, matrix products: 36.6 us -> none  [the longest x3 17.3 us: add_rows(): return jnp.dot(normed, piece, preferred_element_type=jnp.float32)]
    reshape x9 -> x0, local copies, waits for them, and re-layouts: 17.5 us -> none  [the longest x3 16.9 us: finish(): jnp.einsum('hgqk,khd->qhgd', probs, values, preferred_element_type=jnp.fl...]
    convert_element_type x3 -> x0, other arithmetic: 8.26 us -> none  [finish(): return (xf + mixed).astype(jnp.bfloat16)]
    sub x3 -> x0, other arithmetic: 7.08 us -> none  [finish(): expo = jnp.exp(scores - topmost)]
  transfers between devices with their start and end apart: 8 -> 0, of which waited for: 6 -> 0; matrix products, arithmetic and copies ran while one was open for 12% -> 0% of each run, Pallas kernels for 0% -> 0%
where the time goes in v1:
time: 182 us; the launch traced here: 181 us
  Pallas kernels  177 us (97%)
  local copies, waits for them, and re-layouts  3.13 us (2%)
    pallas_call x1, Pallas kernels, per_device(): pl.pallas_call(kernel, out_shape=jax.ShapeDtypeStruct(activations.shape,...  177 us

profile of v1, /device:TPU:8, one launch (start us, length us, event | category | flops | bytes accessed | tf_op | source)
XLA Modules:
  0.0 181.2 jit_solution(11287199195884059053)
XLA Ops:
  0.7 177.4 %relay.1 = bf16[1,1,256,4096]{3,2,1,0:T(8,128)(2,1)} custom-call(bf16[1,1,256,4096]{3,2,1,0:T(8,128)(2,1)} %x_hbm.1, f32[2,1,4096]{2,1,0:T(1,128)} %gains_hbm.1, bf16[2,1,256,1024]{3,2,1,0:T(8,128)(2,1)} %w_hbm.1, s32[1,1]{1,0:T(1,128)S(6)} %copy.6.len_ref), custom_call_target="tpu_custom_call" | custom-call | tf_op jit(solution)/shard_map/relay/pallas_call | solution.py:350
  178.0 3.1 %copy.7 = bf16[1,1,256,4096]{3,2,1,0:T(8,128)(2,1)} copy(bf16[1,1,256,4096]{3,2,1,0:T(8,128)(2,1)} %relay.1) | data formatting | bytes 4194304

commit v2 on v1

--- a/solution.py
+++ b/solution.py
@@ -20,7 +20,7 @@
 def kernel(
     x_hbm, gains_hbm, w_hbm, len_ref, out_hbm,
     wbuf, stage, xbuf, nbuf, gbuf, lbuf, lown, bias, kbuf, vbuf,
-    stage_sem, ring_send, ring_recv, seed_send, x_send, x_recv,
+    stage_sem, ring_send, ring_recv, seed_send, cross_send, x_send, x_recv,
     g_send, g_recv, l_send, l_recv, out_sem,
 ):
     sections = lax.axis_size("section")
@@ -33,11 +33,14 @@
     rows = stage.shape[2]
     nxt = lax.rem(sec + 1, sections)
     prv = lax.rem(sec + sections - 1, sections)
-    across = RING - base + z
+    here = base // RING
+    there = 1 - here
+    across = there * RING + z
     up = base + lax.rem(z + 1, RING)
     down = base + lax.rem(z + RING - 1, RING)
     gives_second = sec <= 1
     has_second = (sec == 1) | (sec == 2)
+    direct = jnp.where(lax.rem(sec, 8) >= 6, 1, 2)
 
     def stage_copy(r, h, part):
         return pltpu.make_async_copy(
@@ -59,20 +62,31 @@
     lown[...] = jnp.full(lown.shape, len_ref[0, 0], jnp.int32)
 
     barrier = pltpu.get_barrier_semaphore()
-    for peer in ((nxt, dp), (nxt, across), (prv, dp), (prv, across), (sec, up), (sec, down)):
+    for peer in ((nxt, dp), (prv, dp), (sec, across), (sec, up), (sec, down)):
         pl.semaphore_signal(barrier, inc=1, device_id=peer, device_id_type=MESH)
-    pl.semaphore_wait(barrier, 6)
+    pl.semaphore_wait(barrier, 5)
 
     def block(ref, r, h, blk):
         return ref.at[r, h, pl.ds(pl.multiple_of(blk * rows, rows), rows), :]
 
-    def seed(r, h, side):
+    def seed(r, h):
         return pltpu.make_async_remote_copy(
             src_ref=stage.at[r, h],
             dst_ref=block(wbuf, r, h, dp),
-            send_sem=seed_send.at[r, h, side],
+            send_sem=seed_send.at[r, h],
             recv_sem=ring_recv.at[r, h, dp],
-            device_id=(nxt, across if side else dp),
+            device_id=(nxt, dp),
+            device_id_type=MESH,
+        )
+
+    def cross(r, h, half, k, way):
+        blk = half * RING + lax.rem(z + (k if way else RING - k), RING)
+        return pltpu.make_async_remote_copy(
+            src_ref=block(wbuf, r, h, blk),
+            dst_ref=block(wbuf, r, h, blk),
+            send_sem=cross_send.at[r, way, h, k],
+            recv_sem=ring_recv.at[r, h, blk],
+            device_id=(sec, across),
             device_id_type=MESH,
         )
 
@@ -87,56 +101,117 @@
             device_id_type=MESH,
         )
 
-    def step(r, group, k):
-        def one(q, carry):
-            h = group * 2 + q // 2
-            half = lax.rem(q, 2)
+    def step_a(r, k):
+        def one(h, carry):
             if k == 0:
-                ring(r, h, half, 0, 0).wait_recv()
+                ring(r, h, here, 0, 0).wait_recv()
+                ring(r, h, here, 0, 0).start()
+                ring(r, h, here, 0, 1).start()
+                cross(r, h, here, 0, 0).start()
+            elif k < 4:
+                for way in range(2):
+                    ring(r, h, here, k, way).wait_recv()
+                    if k < 3:
+                        ring(r, h, here, k, way).start()
+                    else:
+
+                        @pl.when(h == way)
+                        def _():
+                            ring(r, h, here, k, way).start()
+
+                    cross(r, h, here, k, way).start()
+            else:
+                ring(r, h, here, k, 0).wait_recv()
+                cross(r, h, here, k, 0).start()
+            return carry
+
+        lax.fori_loop(0, direct, one, 0)
+
+    def landed(r, h):
+        ring(r, h, there, 0, 0).wait_recv()
+        for k in range(1, 4):
+            ring(r, h, there, k, 0).wait_recv()
+            ring(r, h, there, k, 1).wait_recv()
+        ring(r, h, there, 4, 0).wait_recv()
+
+    def cross_b(r):
+        def one(h, carry):
+            ring(r, h, here, 0, 0).wait_recv()
+            cross(r, h, here, 0, 0).start()
+            return carry
+
+        lax.fori_loop(direct, KV_HEADS, one, 0)
+
+    def step_b(r, h, k):
+        def one(second, carry):
+            half = jnp.where(second == 0, here, there)
+            if k == 0:
+
+                @pl.when(second == 1)
+                def _():
+                    ring(r, h, half, 0, 0).wait_recv()
+
                 ring(r, h, half, 0, 0).start()
                 ring(r, h, half, 0, 1).start()
-            elif k < 3:
-                ring(r, h, half, k, 0).wait_recv()
-                ring(r, h, half, k, 0).start()
-                ring(r, h, half, k, 1).wait_recv()
-                ring(r, h, half, k, 1).start()
-            elif k == 3:
-                ring(r, h, half, k, 0).wait_recv()
-
-                @pl.when(lax.rem(h, 2) == 0)
-                def _():
-                    ring(r, h, half, k, 0).start()
-
-                ring(r, h, half, k, 1).wait_recv()
-
-                @pl.when(lax.rem(h, 2) == 1)
-                def _():
-                    ring(r, h, half, k, 1).start()
+            elif k < 4:
+                for way in range(2):
+                    ring(r, h, half, k, way).wait_recv()
+                    if k < 3:
+                        ring(r, h, half, k, way).start()
+                    else:
+
+                        @pl.when(lax.rem(h + second, 2) == way)
+                        def _():
+                            ring(r, h, half, k, way).start()
+
             else:
                 ring(r, h, half, k, 0).wait_recv()
             return carry
 
-        lax.fori_loop(0, 4, one, 0)
-
-    def ring_done(r):
-        def one(q, carry):
-            h = q // 2
-            half = lax.rem(q, 2)
-            for k in range(3):
-                ring(r, h, half, k, 0).wait_send()
-                ring(r, h, half, k, 1).wait_send()
-
-            @pl.when(lax.rem(h, 2) == 0)
-            def _():
-                ring(r, h, half, 3, 0).wait_send()
-
-            @pl.when(lax.rem(h, 2) == 1)
-            def _():
-                ring(r, h, half, 3, 1).wait_send()
-
+        lax.fori_loop(0, 2, one, 0)
+
+    def slot(r, n):
+        for m in range(KV_HEADS - 1):
+            if 0 <= n - 2 * m <= 4:
+
+                @pl.when(direct + m < KV_HEADS)
+                def _():
+                    step_b(r, direct + m, n - 2 * m)
+
+    def pair(r, k):
+        step_b(r, 2, k)
+        step_b(r, 3, k)
+
+    def ring_sent(r, h, half, last):
+        for k in range(3):
+            ring(r, h, half, k, 0).wait_send()
+            ring(r, h, half, k, 1).wait_send()
+
+        @pl.when(last == 0)
+        def _():
+            ring(r, h, half, 3, 0).wait_send()
+
+        @pl.when(last == 1)
+        def _():
+            ring(r, h, half, 3, 1).wait_send()
+
+    def all_sent(r):
+        def one_a(h, carry):
+            ring_sent(r, h, here, lax.rem(h, 2))
+            for k in range(5):
+                cross(r, h, here, k, 0).wait_send()
+            for k in range(1, 4):
+                cross(r, h, here, k, 1).wait_send()
             return carry
 
-        lax.fori_loop(0, 2 * KV_HEADS, one, 0)
+        def one_b(h, carry):
+            ring_sent(r, h, here, lax.rem(h, 2))
+            ring_sent(r, h, there, lax.rem(h + 1, 2))
+            cross(r, h, here, 0, 0).wait_send()
+            return carry
+
+        lax.fori_loop(0, direct, one_a, 0)
+        lax.fori_loop(direct, KV_HEADS, one_b, 0)
 
     def first_x(c):
         return pltpu.make_async_remote_copy(
@@ -180,11 +255,22 @@
             out_sem.at[c],
         )
 
-    for h in range(KV_HEADS):
-        for part in range(2):
-            stage_copy(0, h, part).wait()
-        seed(0, h, 0).start()
-        seed(0, h, 1).start()
+    def seeds(r, heads):
+        for h in heads:
+            for part in range(2):
+                stage_copy(r, h, part).wait()
+            seed(r, h).start()
+
+    vbuf[:, HEAD_DIM:] = jnp.ones((seq, HEAD_DIM), jnp.bfloat16)
+
+    seeds(0, (0, 1))
+    step_a(0, 0)
+    for h in (0, 1):
+        seed(0, h).wait_send()
+    seeds(0, (2, 3))
+    cross_b(0)
+    for h in (2, 3):
+        seed(0, h).wait_send()
     move_gains.start()
     shift_len(0, lown).start()
     for c in range(KV_HEADS):
@@ -192,19 +278,14 @@
 
     @pl.when(gives_second)
     def _():
-        for h in range(KV_HEADS):
-            for part in range(2):
-                stage_copy(1, h, part).wait()
-            seed(1, h, 0).start()
-            seed(1, h, 1).start()
-
-    vbuf[:, HEAD_DIM:] = jnp.ones((seq, HEAD_DIM), jnp.bfloat16)
-
-    step(0, 0, 0)
-    step(0, 0, 1)
-    step(0, 0, 2)
-    step(0, 1, 0)
-    step(0, 0, 3)
+        seeds(1, range(KV_HEADS))
+
+    step_a(0, 1)
+    step_a(0, 2)
+    slot(0, 0)
+    step_a(0, 3)
+    step_a(0, 4)
+    slot(0, 1)
     move_gains.wait_recv()
 
     def one_head(i, carry):
@@ -212,31 +293,44 @@
         h = lax.rem(i, KV_HEADS)
         r = ((sec >= 1) & (t >= sec)).astype(jnp.int32)
 
+        def both(first, second):
+            return ((sec == 1) & (i == first)) | ((sec == 2) & (i == second))
+
         @pl.when(i == 1)
         def _():
-            step(0, 1, 2)
-
-        @pl.when(i == 2)
-        def _():
-            step(0, 1, 3)
-
-            @pl.when(has_second)
-            def _():
-                step(1, 0, 0)
-                step(1, 1, 0)
-
-            step(0, 1, 4)
-
-        @pl.when((i == KV_HEADS) & has_second)
-        def _():
-            step(1, 0, 1)
-            step(1, 1, 1)
-
-        @pl.when(((i == KV_HEADS) & (sec == 1)) | ((i == 2 * KV_HEADS) & (sec == 2)))
-        def _():
-            for k in range(2, 5):
-                step(1, 0, k)
-                step(1, 1, k)
+            slot(0, 5)
+
+        @pl.when(i == direct + 1)
+        def _():
+            slot(0, 6)
+
+        @pl.when(i == 3)
+        def _():
+            slot(0, 7)
+            slot(0, 8)
+
+        @pl.when((i == 2) & has_second)
+        def _():
+            step_a(1, 0)
+            cross_b(1)
+
+        @pl.when((i == 3) & has_second)
+        def _():
+            step_a(1, 1)
+
+        @pl.when((i == 4) & has_second)
+        def _():
+            step_a(1, 2)
+            pair(1, 0)
+
+        @pl.when(both(4, 4))
+        def _():
+            step_a(1, 3)
+            step_a(1, 4)
+
+        @pl.when(both(4, 5))
+        def _():
+            pair(1, 1)
 
         @pl.when(h == 0)
         def _():
@@ -274,16 +368,33 @@
 
         @pl.when(i == 0)
         def _():
-            step(0, 0, 4)
-            step(0, 1, 1)
+            slot(0, 2)
+            slot(0, 3)
+            slot(0, 4)
+
+        @pl.when(both(4, 6))
+        def _():
+            pair(1, 2)
+
+        @pl.when(both(5, 7))
+        def _():
+            pair(1, 3)
+
+        @pl.when(both(6, 10))
+        def _():
+            pair(1, 4)
+
+        @pl.when((h < direct) & ((t == 0) | (t == sec)))
+        def _():
+            landed(r, h)
 
         keyval = jnp.dot(nbuf[...], wbuf[r, h], preferred_element_type=jnp.float32)
         kbuf[...] = keyval[:, :HEAD_DIM].astype(jnp.bfloat16)
         vbuf[:, :HEAD_DIM] = keyval[:, HEAD_DIM:].astype(jnp.bfloat16)
 
-        def heads(pair, carry):
+        def heads(part, carry):
             for jj in range(4):
-                j = pair * 4 + jj
+                j = part * 4 + jj
                 at = pl.ds(pl.multiple_of(h * cols + j * HEAD_DIM, HEAD_DIM), HEAD_DIM)
                 put = pl.ds(pl.multiple_of(j * HEAD_DIM, HEAD_DIM), HEAD_DIM)
                 for half in range(2):
@@ -322,20 +433,16 @@
         first_x(c).wait_send()
         shift_x(1, c).wait_send()
         shift_x(2, c).wait_send()
-    for h in range(KV_HEADS):
-        seed(0, h, 0).wait_send()
-        seed(0, h, 1).wait_send()
-    ring_done(0)
+    all_sent(0)
 
     @pl.when(gives_second)
     def _():
         for h in range(KV_HEADS):
-            seed(1, h, 0).wait_send()
-            seed(1, h, 1).wait_send()
+            seed(1, h).wait_send()
 
     @pl.when(has_second)
     def _():
-        ring_done(1)
+        all_sent(1)
 
     for c in range(KV_HEADS):
         write(c).wait()
@@ -371,7 +478,8 @@
             dma((2, KV_HEADS, 2)),
             dma((2, 2, KV_HEADS, 2, 5)),
             dma((2, KV_HEADS, blocks)),
-            dma((2, KV_HEADS, 2)),
+            dma((2, KV_HEADS)),
+            dma((2, 2, KV_HEADS, 5)),
             dma((TICKS, KV_HEADS)),
             dma((TICKS, KV_HEADS)),
             dma, dma,

time: 182 us -> 150 us (0.82)
  Pallas kernels: 177 us -> 146 us
    pallas_call x1, Pallas kernels: 177 us -> 146 us  [per_device(): pl.pallas_call(kernel, out_shape=jax.ShapeDtypeStruct(activations.shape,...]
where the time goes in v2:
time: 150 us
  Pallas kernels  146 us (97%)
  local copies, waits for them, and re-layouts  3.13 us (2%)
    pallas_call x1, Pallas kernels, per_device(): pl.pallas_call(kernel, out_shape=jax.ShapeDtypeStruct(activations.shape,...  146 us
    unnamed x1, local copies, waits for them, and re-layouts  3.13 us

profile of v2, /device:TPU:8, one launch (start us, length us, event | category | flops | bytes accessed | tf_op | source)
XLA Modules:
  0.0 150.0 jit_solution(11329987610966622967)
XLA Ops:
  0.7 146.2 %relay.1 = bf16[1,1,256,4096]{3,2,1,0:T(8,128)(2,1)} custom-call(bf16[1,1,256,4096]{3,2,1,0:T(8,128)(2,1)} %x_hbm.1, f32[2,1,4096]{2,1,0:T(1,128)} %gains_hbm.1, bf16[2,1,256,1024]{3,2,1,0:T(8,128)(2,1)} %w_hbm.1, s32[1,1]{1,0:T(1,128)S(6)} %copy.6.len_ref), custom_call_target="tpu_custom_call" | custom-call | tf_op jit(solution)/shard_map/relay/pallas_call | solution.py:457
  146.9 3.1 %copy.7 = bf16[1,1,256,4096]{3,2,1,0:T(8,128)(2,1)} copy(bf16[1,1,256,4096]{3,2,1,0:T(8,128)(2,1)} %relay.1) | data formatting | bytes 4194304

commit v3 on v2

--- a/solution.py
+++ b/solution.py
@@ -392,24 +392,36 @@
         kbuf[...] = keyval[:, :HEAD_DIM].astype(jnp.bfloat16)
         vbuf[:, :HEAD_DIM] = keyval[:, HEAD_DIM:].astype(jnp.bfloat16)
 
+        todo = [(jj, half) for jj in range(4) for half in range(2)]
+
+        def span(half):
+            return slice(half * seq // 2, (half + 1) * seq // 2), (half + 1) * seq // 2
+
         def heads(part, carry):
-            for jj in range(4):
-                j = part * 4 + jj
-                at = pl.ds(pl.multiple_of(h * cols + j * HEAD_DIM, HEAD_DIM), HEAD_DIM)
-                put = pl.ds(pl.multiple_of(j * HEAD_DIM, HEAD_DIM), HEAD_DIM)
-                for half in range(2):
-                    mine = slice(half * seq // 2, (half + 1) * seq // 2)
-                    seen = (half + 1) * seq // 2
-                    scores = lax.dot_general(
-                        nbuf[mine, at], kbuf[:seen, :], (((1,), (1,)), ((), ())),
+            def place(jj, start):
+                at = start + (part * 4 + jj) * HEAD_DIM
+                return pl.ds(pl.multiple_of(at, HEAD_DIM), HEAD_DIM)
+
+            scored = []
+            for jj, half in todo:
+                mine, seen = span(half)
+                scored.append(
+                    lax.dot_general(
+                        nbuf[mine, place(jj, h * cols)], kbuf[:seen, :], (((1,), (1,)), ((), ())),
                         preferred_element_type=jnp.float32,
                     ) + bias[mine, :seen]
-                    top = jnp.max(scores, axis=-1, keepdims=True)
-                    expo = jnp.exp2((scores - top) * SCALE2).astype(jnp.bfloat16)
-                    both = jnp.dot(expo, vbuf[:seen, :], preferred_element_type=jnp.float32)
-                    mixed = both[:, :HEAD_DIM] / both[:, HEAD_DIM:]
-                    old = xbuf[t, h, mine, put].astype(jnp.float32)
-                    xbuf[t, h, mine, put] = (old + mixed).astype(jnp.bfloat16)
+                )
+            weights = []
+            for scores in scored:
+                top = jnp.max(scores, axis=-1, keepdims=True)
+                weights.append(jnp.exp2((scores - top) * SCALE2).astype(jnp.bfloat16))
+            for (jj, half), expo in zip(todo, weights):
+                mine, seen = span(half)
+                put = place(jj, 0)
+                summed = jnp.dot(expo, vbuf[:seen, :], preferred_element_type=jnp.float32)
+                mixed = summed[:, :HEAD_DIM] / summed[:, HEAD_DIM:]
+                old = xbuf[t, h, mine, put].astype(jnp.float32)
+                xbuf[t, h, mine, put] = (old + mixed).astype(jnp.bfloat16)
             return carry
 
         lax.fori_loop(0, PER_KV // 4, heads, 0)

time: 150 us -> 146 us (0.973)
  Pallas kernels: 146 us -> 142 us
    pallas_call x1, Pallas kernels: 146 us -> 142 us  [per_device(): pl.pallas_call(kernel, out_shape=jax.ShapeDtypeStruct(activations.shape,...]
where the time goes in v3:
time: 146 us
  Pallas kernels  142 us (97%)
  local copies, waits for them, and re-layouts  3.13 us (2%)
    pallas_call x1, Pallas kernels, per_device(): pl.pallas_call(kernel, out_shape=jax.ShapeDtypeStruct(activations.shape,...  142 us
    unnamed x1, local copies, waits for them, and re-layouts  3.13 us

profile of v3, /device:TPU:8, one launch (start us, length us, event | category | flops | bytes accessed | tf_op | source)
XLA Modules:
  0.0 145.7 jit_solution(8864288807335329961)
XLA Ops:
  0.7 141.9 %relay.1 = bf16[1,1,256,4096]{3,2,1,0:T(8,128)(2,1)} custom-call(bf16[1,1,256,4096]{3,2,1,0:T(8,128)(2,1)} %x_hbm.1, f32[2,1,4096]{2,1,0:T(1,128)} %gains_hbm.1, bf16[2,1,256,1024]{3,2,1,0:T(8,128)(2,1)} %w_hbm.1, s32[1,1]{1,0:T(1,128)S(6)} %copy.6.len_ref), custom_call_target="tpu_custom_call" | custom-call | tf_op jit(solution)/shard_map/relay/pallas_call | solution.py:469
  142.6 3.1 %copy.7 = bf16[1,1,256,4096]{3,2,1,0:T(8,128)(2,1)} copy(bf16[1,1,256,4096]{3,2,1,0:T(8,128)(2,1)} %relay.1) | data formatting | bytes 4194304
